TPU v7x, 128 devices: a whole 4x4x4 slice. The times are simulated.
128 devices in a mesh: gx: 16 (over y, x), gy: 8 (over z, core).
Axes of the slice: x: 4, y: 4, z: 4, core: 2. Of those that a mesh axis runs over, the one named last changes fastest.
Arguments:
- coarse_source: float32 [512, 8192], P('gx', 'gy'), may hold values from -6 to 6
- coarse_coefficient: float32 [512, 8192], P('gx', 'gy'), may hold values from 0.25 to 4
- coarse_start: float32 [512, 8192], P('gx', 'gy'), may hold values from -6 to 6
- fine_source: float32 [128, 32, 1024], P(('gx', 'gy')), may hold values from -6 to 6
- fine_coefficient: float32 [128, 32, 1024], P(('gx', 'gy')), may hold values from 0.25 to 4
- fine_start: float32 [128, 32, 1024], P(('gx', 'gy')), may hold values from -6 to 6
- fine_position: int32 [128], replicated, may hold values from 0 to 1023, as said below
- first_colour: int32 [3], replicated, may hold values from 0 to 1
Outputs:
- coarse_solution: float32 [512, 8192], P('gx', 'gy')
- fine_solution: float32 [128, 32, 1024], P(('gx', 'gy'))
Inputs may be any that keep to these rules, and one draw needn't show every extreme that they name: `fine_position`: entry r is the box held by device r = gx index * 8 + gy index; its coarse device p // 8 has the same gy index as device r; only octants whose three bits sum to an even number occur, so no two boxes share a face; positions are distinct; in every gy index some coarse device lies under four boxes, and some box lies 16 // 2 gx indices away from its coarse device.
All inputs are finite; a program needn't handle non-finite values.
Results may differ from a plain program's by a relative error of at most 0.0003.
Values sent between devices are 32-bit elements; how exact they have to be, the bound alone decides.
A program may use at most 64 MiB of HBM per device.

v0:
```python
import functools

import jax
import jax.numpy as jnp
from jax import lax
from jax.experimental import pallas as pl
from jax.experimental.pallas import tpu as pltpu
from jax.sharding import PartitionSpec as P


MESH = pl.DeviceIdType.MESH
F32 = jnp.float32
BF16 = jnp.bfloat16
SWEEPS = 4
N_X = 16
N_Y = 8


def iota(shape, dim):
    return lax.broadcasted_iota(jnp.int32, shape, dim)


def halves(values):
    high = values.astype(BF16)
    low = (values - high.astype(F32)).astype(BF16)
    return jnp.concatenate([high, low], axis=0)


def mapped(values, matrix):
    rows = values.shape[0]
    both = jnp.dot(halves(values), matrix, preferred_element_type=F32)
    return both[:rows] + both[rows:]


def roll(values, amount):
    return pltpu.roll(values, amount, axis=1)


def y_before(ref, j, rows, lanes, step):
    return roll(jnp.where(lanes >= 128 - step, ref[j - 1, rows], ref[j, rows]), step)


def y_beyond(ref, j, rows, lanes, step):
    return roll(jnp.where(lanes < step, ref[j + 1, rows], ref[j, rows]), 128 - step)


def coupled(value, weights, j, low, count, lanes, step):
    wx, wy, wz = weights
    here = pl.ds(low, count)
    before = pl.ds(low - 1, count)
    beyond = pl.ds(low + 1, count)
    mid = value[j, here]
    w_y = wy[j, here]
    w_z = wz[j, here]
    total = wx[j, here] * value[j, before] + wx[j, beyond] * value[j, beyond]
    total = total + w_y * y_before(value, j, here, lanes, step)
    ahead = jnp.where(lanes < step, wy[j + 1, here] * value[j + 1, here], w_y * mid)
    total = total + roll(ahead, 128 - step)
    return total + w_z * roll(mid, 1) + roll(w_z * mid, 127)


def zero_pads(ref, low, high):
    blocks, rows, _ = ref.shape
    ref[0] = jnp.zeros((rows, 128), F32)
    ref[blocks - 1] = jnp.zeros((rows, 128), F32)
    ref[1 : blocks - 1, :low] = jnp.zeros((blocks - 2, low, 128), F32)
    ref[1 : blocks - 1, high:] = jnp.zeros((blocks - 2, rows - high, 128), F32)


def put(ref, mask):
    ref[...] = jnp.where(mask, 1.0, 0.0).astype(BF16)


def kernel(
    pos,
    colours,
    c_source,
    c_coeff,
    c_start,
    f_source,
    f_coeff,
    f_start,
    out_c,
    out_f,
    s_fr,
    kq_fr,
    src_c,
    f_src,
    f_k,
    f_v,
    f_wx,
    f_wy,
    f_wz,
    f_inv,
    f_base,
    f_a,
    f_sm,
    f_d,
    f_res,
    f_gx,
    k_fr,
    r_fr,
    wx,
    wy,
    wz,
    inv_a,
    inv_b,
    e_a,
    e_b,
    left,
    b_k,
    b_wx,
    b_wy,
    b_wz,
    b_ia,
    b_ib,
    b_fa,
    b_fb,
    b_ua,
    b_ub,
    x_rows,
    faces,
    ghost_out,
    ghost_in,
    box_out,
    box_in,
    boxes,
    e_oct,
    e_out,
    e_in,
    u_oct,
    u_out,
    u_in,
    dup,
    dup2,
    m_face,
    m_ghost,
    m_down,
    m_up,
    m_exp,
    m_com,
    m_four,
    sem_l,
    sem_s0,
    sem_r0,
    sem_sk,
    sem_rk,
    sem_sr,
    sem_rr,
    sem_s1,
    sem_r1,
    sem_s2,
    sem_r2,
    sem_s3,
    sem_r3,
    sem_s4,
    sem_r4,
    sem_s5,
    sem_r5,
):
    mx = lax.axis_index("gx")
    my = lax.axis_index("gy")
    x_up, x_dn = lax.rem(mx + 1, N_X), lax.rem(mx + N_X - 1, N_X)
    y_up, y_dn = lax.rem(my + 1, N_Y), lax.rem(my + N_Y - 1, N_Y)
    around = [
        (x_dn, my),
        (x_up, my),
        (mx, y_dn),
        (mx, y_up),
        (x_dn, y_dn),
        (x_dn, y_up),
        (x_up, y_dn),
        (x_up, y_up),
    ]
    mates = [(lax.rem(mx + d, N_X), my) for d in range(1, N_X)]

    barrier = pltpu.get_barrier_semaphore()
    greeted = mates + around[2:]
    for device in greeted:
        pl.semaphore_signal(barrier, inc=1, device_id=device, device_id_type=MESH)

    loads = []

    def load(number, source, target):
        group = []
        for j in range(8):
            copy = pltpu.make_async_copy(source(j), target(j), sem_l.at[number, j])
            copy.start()
            group.append(copy)
        loads.append(group)

    def chunk(j):
        return pl.ds(128 * j, 128)

    load(0, lambda j: c_start.at[:, chunk(j)], lambda j: s_fr.at[1 + j, pl.ds(8, 32)])
    load(1, lambda j: c_coeff.at[:, chunk(j)], lambda j: kq_fr.at[1 + j, pl.ds(8, 32)])
    load(2, lambda j: f_coeff.at[0, :, chunk(j)], lambda j: f_k.at[1 + j, pl.ds(8, 32)])
    load(3, lambda j: f_start.at[0, :, chunk(j)], lambda j: f_v.at[1 + j, pl.ds(8, 32)])
    load(4, lambda j: f_source.at[0, :, chunk(j)], lambda j: f_src.at[j])
    load(5, lambda j: c_source.at[:, chunk(j)], lambda j: src_c.at[j])
    load(6, lambda j: c_coeff.at[:, chunk(j)], lambda j: k_fr.at[5 + j, pl.ds(24, 32)])

    own_pos = pos[mx * N_Y + my]
    owner_x = own_pos >> 6
    own_oz = own_pos & 1

    slots = []
    for ye in range(4):
        row = (my, y_dn, y_up)[1 if ye == 0 else (2 if ye == 3 else 0)]
        for sx in range(4):
            ox, oy = (sx + 1) % 2, (ye + 1) % 2
            octant = 4 * ox + 2 * oy + (ox + oy) % 2
            column = mx + (-1, 0, 0, 1)[sx]
            slots.append((row, (column * N_Y + row) * 8 + octant))

    def look(h, found):
        held = [pos[h * N_Y + row] for row in (my, y_dn, y_up)]
        result = []
        for number, (row, wanted) in enumerate(slots):
            ye = number // 4
            at = held[1 if ye == 0 else (2 if ye == 3 else 0)]
            result.append(jnp.where(at == wanted, h, found[number]))
        return tuple(result)

    found = lax.fori_loop(0, N_X, look, tuple(jnp.int32(-1) for _ in slots))
    octs = [(pos[h * N_Y + my] >> 1) & 3 for h in range(N_X)]

    lanes = iota((1, 128), 1)
    z_first = lanes % 32 == 0
    z_last = lanes % 32 == 31
    parity = (iota((8, 128), 0) + iota((8, 128), 1) // 32 + iota((8, 128), 1)) % 2
    parity_b = (iota((8, 128), 0) + iota((8, 128), 1) // 16 + iota((8, 128), 1)) % 2

    def painted(base, colour, rows):
        flags = jnp.where(base == colour, 1.0, 0.0)
        return jnp.concatenate([flags] * (rows // 8), axis=0) > 0.5

    first_f = painted(parity, colours[0], 32)
    first_c = painted(parity, colours[1], 64)
    first_b = painted(parity_b, colours[2], 32)

    zero_pads(f_v, 8, 40)
    zero_pads(f_wx, 8, 40)
    zero_pads(f_wy, 8, 40)
    zero_pads(f_a, 8, 40)
    zero_pads(f_d, 8, 40)
    x_rows[...] = jnp.zeros(x_rows.shape, F32)
    f_gx[...] = jnp.zeros(f_gx.shape, F32)

    for oz in range(2):
        k = iota((896, 128), 0)
        c = iota((896, 128), 1)
        block, lane = k // 128, k % 128
        z, yy = lane % 32, lane // 32
        mask = (block == 0) & (c < 16) & (lane == 96 + 16 * oz + c)
        mask = mask | ((block == 1) & (c >= 16) & (c < 32) & (lane == 16 * oz + c - 16))
        own = (block >= 2) & (block < 6) & (z == (16, 15)[oz])
        mask = mask | (own & (c == (48, 32)[oz] + 4 * (block - 2) + yy))
        mask = mask | (
            (block == 6) & (z >= 16 * oz) & (z < 16 * oz + 16) & (c == 64 + yy * 16 + z - 16 * oz)
        )
        m_face[oz] = jnp.where(mask, 1.0, 0.0).astype(BF16)

    for group in loads[:2]:
        for copy in group:
            copy.wait()
    pl.semaphore_wait(barrier, len(greeted))

    sends = []

    def remote(source, target, send_sem, recv_sem, device):
        copy = pltpu.make_async_remote_copy(
            src_ref=source,
            dst_ref=target,
            send_sem=send_sem,
            recv_sem=recv_sem,
            device_id=device,
            device_id_type=MESH,
        )
        copy.start()
        sends.append(copy)
        return copy

    layer = []
    for number, ref in enumerate((s_fr, kq_fr)):
        rows, blocks = pl.ds(8, 32), pl.ds(1, 8)
        for side, (source, target, device) in enumerate(
            (
                (ref.at[8, rows], ref.at[0, rows], around[3]),
                (ref.at[1, rows], ref.at[9, rows], around[2]),
                (ref.at[blocks, pl.ds(39, 1)], ref.at[blocks, pl.ds(7, 1)], around[1]),
                (ref.at[blocks, pl.ds(8, 1)], ref.at[blocks, pl.ds(40, 1)], around[0]),
            )
        ):
            at = 4 * number + side
            layer.append(remote(source, target, sem_s0.at[at], sem_r0.at[at], device))

    for group in loads[2:5]:
        for copy in group:
            copy.wait()
    rows_f = iota((32, 128), 0)
    own_f = pl.ds(8, 32)

    def fine_weights(i, carry):
        j = i + 1
        k = f_k[j, own_f]
        y_first = (lanes < 32) & (j == 1)
        y_last = (lanes >= 96) & (j == 8)
        kxm = jnp.where(rows_f == 0, k, f_k[j, pl.ds(7, 32)])
        kxp = jnp.where(rows_f == 31, k, f_k[j, pl.ds(9, 32)])
        kym = jnp.where(y_first, k, y_before(f_k, j, own_f, lanes, 32))
        kyp = jnp.where(y_last, k, y_beyond(f_k, j, own_f, lanes, 32))
        kzm = jnp.where(z_first, k, roll(k, 1))
        kzp = jnp.where(z_last, k, roll(k, 127))
        f_wx[j, own_f] = jnp.where(rows_f == 0, 0.0, 0.5 * (k + kxm))
        f_wy[j, own_f] = jnp.where(y_first, 0.0, 0.5 * (k + kym))
        f_wz[j, own_f] = jnp.where(z_first, 0.0, 0.5 * (k + kzm))
        f_inv[j, own_f] = 1.0 / (3.0 * k + 0.5 * (kxm + kxp + kym + kyp + kzm + kzp))
        return carry

    lax.fori_loop(0, 8, fine_weights, 0)
    w_f = (f_wx, f_wy, f_wz)

    def fine_base(i, carry):
        f_base[i + 1, own_f] = 0.25 * f_src[i] + coupled(f_v, w_f, i + 1, 8, 32, lanes, 32)
        return carry

    lax.fori_loop(0, 8, fine_base, 0)

    for copy in layer:
        copy.wait_recv()
    for ref in (s_fr, kq_fr):

        @pl.when(mx == 0)
        def _():
            ref[1:9, 7:8] = jnp.zeros((8, 1, 128), F32)

        @pl.when(mx == N_X - 1)
        def _():
            ref[1:9, 40:41] = jnp.zeros((8, 1, 128), F32)

        @pl.when(my == 0)
        def _():
            ref[0, 8:40] = jnp.zeros((32, 128), F32)

        @pl.when(my == N_Y - 1)
        def _():
            ref[9, 8:40] = jnp.zeros((32, 128), F32)

    for ox in range(2):
        for oy in range(2):
            for q in range(4):
                for at, row in ((q, 7 + 16 * ox), (4 + q, 24 + 16 * ox)):
                    x_rows[2 * ox + oy, at : at + 1] = s_fr[1 + 4 * oy + q, row : row + 1]
    for oz in range(2):
        pair = [(0, oz), (1, 1 - oz)]
        stacked = []
        for ox, oy in pair:
            rows = pl.ds(8 + 16 * ox, 16)
            parts = [s_fr[4 * oy, rows], s_fr[5 + 4 * oy, rows]]
            parts += [s_fr[1 + 4 * oy + q, rows] for q in range(4)]
            parts.append(x_rows[2 * ox + oy])
            stacked.append(jnp.concatenate(parts, axis=1))
        packed = mapped(jnp.concatenate(stacked, axis=0), m_face[oz])
        for number, (ox, oy) in enumerate(pair):
            faces[2 * ox + oy] = packed[16 * number : 16 * number + 16]

    def to_mates(source, target, send_sem, recv_sem):
        started = []
        for d in range(1, N_X):
            other = lax.rem(mx + d, N_X)
            started.append(
                remote(source(other), target.at[mx], send_sem.at[d], recv_sem.at[d], (other, my))
            )
        return started

    for h in range(N_X):
        ghost_out[h] = faces[octs[h]]
    ghosts = to_mates(lambda other: ghost_out.at[other], ghost_in, sem_s1, sem_r1)
    ghost_in[mx] = ghost_out[mx]

    for copy in loads[6]:
        copy.wait()

    def deep(ref, base, width, blocks, send_sem, recv_sem):
        full_r, full_b = (base, base, 32), (5, 5, 8)
        r_low = (base, base + 32, width)
        r_high = (base + 32 - width, base - width, width)
        b_low = (5, 13, blocks)
        b_high = (13 - blocks, 5 - blocks, blocks)
        started = []
        for number, (r, b) in enumerate(
            (
                (r_low, full_b),
                (r_high, full_b),
                (full_r, b_low),
                (full_r, b_high),
                (r_low, b_low),
                (r_low, b_high),
                (r_high, b_low),
                (r_high, b_high),
            )
        ):
            started.append(
                remote(
                    ref.at[pl.ds(b[0], b[2]), pl.ds(r[0], r[2])],
                    ref.at[pl.ds(b[1], b[2]), pl.ds(r[1], r[2])],
                    send_sem.at[number],
                    recv_sem.at[number],
                    around[number],
                )
            )
        return started

    deep_k = deep(k_fr, 24, 24, 5, sem_sk, sem_rk)

    for copy in loads[5]:
        copy.wait()

    def coarse_residual(i, carry):
        j = i + 1
        s = s_fr[j, own_f]
        k = kq_fr[j, own_f]

        def flux(k_there, s_there):
            return (k + k_there) * (s - s_there)

        before, beyond = pl.ds(7, 32), pl.ds(9, 32)
        total = flux(kq_fr[j, before], s_fr[j, before]) + flux(kq_fr[j, beyond], s_fr[j, beyond])
        total = total + flux(
            y_before(kq_fr, j, own_f, lanes, 32), y_before(s_fr, j, own_f, lanes, 32)
        )
        total = total + flux(
            y_beyond(kq_fr, j, own_f, lanes, 32), y_beyond(s_fr, j, own_f, lanes, 32)
        )
        total = total + flux(
            jnp.where(z_first, 0.0, roll(k, 1)), jnp.where(z_first, 0.0, roll(s, 1))
        )
        total = total + flux(
            jnp.where(z_last, 0.0, roll(k, 127)), jnp.where(z_last, 0.0, roll(s, 127))
        )
        r_fr[i + 5, pl.ds(24, 32)] = src_c[i] - 0.5 * total
        return carry

    lax.fori_loop(0, 8, coarse_residual, 0)
    deep_r = deep(r_fr, 24, 16, 4, sem_sr, sem_rr)

    k = iota((128, 1280), 0)
    c = iota((128, 1280), 1)
    y, z = c // 32, c % 32
    inner = c < 1024
    mask = inner & (y == 0) & (k == z // 2)
    mask = mask | (inner & (y == 31) & (k == 16 + z // 2))
    mask = mask | (inner & (z == 0) & (k == 32 + y // 2))
    mask = mask | (inner & (z == 31) & (k == 48 + y // 2))
    mask = mask | ((c >= 1024) & (k == 64 + (y - 32) // 2 * 16 + z // 2))
    put(m_ghost, mask)
    k, c = iota((512, 128), 0), iota((512, 128), 1)
    put(m_down, c == k // 64 * 16 + k % 32 // 2)

    for copy in ghosts:
        copy.wait_recv()
    mine = ghost_in[owner_x]
    dup[0, pl.ds(0, 16, stride=2)] = mine
    dup[0, pl.ds(1, 16, stride=2)] = mine
    widened = mapped(dup[0], m_ghost[...])
    for q in range(4):
        for t in range(2):
            piece = widened[:, 1024 + 128 * t : 1152 + 128 * t]
            f_gx[2 * q + t, 0:1] = piece[2 * q : 2 * q + 1]
            f_gx[2 * q + t, 31:32] = piece[8 + 2 * q : 9 + 2 * q]
    for i in range(8):
        j = i + 1
        ghost = f_k[j, own_f] * (widened[:, 128 * i : 128 * i + 128] + f_gx[i])
        f_gx[i] = ghost
        f_a[j, own_f] = jnp.where(first_f, (f_base[j, own_f] + ghost) * f_inv[j, own_f], 0.0)
    for i in range(8):
        j = i + 1
        around_a = coupled(f_a, w_f, j, 8, 32, lanes, 32)
        fresh = (0.25 * f_src[i] + f_gx[i] + around_a) * f_inv[j, own_f]
        f_sm[i] = jnp.where(first_f, f_a[j, own_f], fresh)
        f_d[j, own_f] = jnp.where(first_f, 0.0, fresh - f_v[j, own_f])
    for i in range(8):
        f_res[i] = jnp.where(first_f, coupled(f_d, w_f, i + 1, 8, 32, lanes, 32), 0.0)
    stacked = []
    for b in range(2):
        parts = [
            f_res[4 * b + q, pl.ds(0, 16, stride=2)] + f_res[4 * b + q, pl.ds(1, 16, stride=2)]
            for q in range(4)
        ]
        stacked.append(jnp.concatenate(parts, axis=1))
    packed = 0.5 * mapped(jnp.concatenate(stacked, axis=0), m_down[...])
    box_out[0] = packed[:16]
    box_out[1] = packed[16:]
    gathered = to_mates(lambda other: box_out, box_in, sem_s2, sem_r2)
    box_in[mx] = box_out[...]

    zero_pads(wx, 8, 72)
    zero_pads(wy, 8, 72)
    zero_pads(e_a, 8, 72)
    zero_pads(e_b, 8, 72)
    for ref in (b_k, b_wx, b_wy, b_ua, b_ub):
        zero_pads(ref, 8, 40)
    for oz in range(2):
        k, c = iota((128, 256), 0), iota((128, 256), 1)
        m_exp[oz] = jnp.where((k // 16 == c // 32) & (c % 32 == 16 * oz + k % 16), 1.0, 0.0).astype(BF16)
        k, c = iota((256, 128), 1), iota((256, 128), 0)
        m_com[oz] = jnp.where((k // 16 == c // 32) & (c % 32 == 16 * oz + k % 16), 1.0, 0.0).astype(BF16)
    k, c = iota((128, 512), 0), iota((128, 512), 1)
    put(m_up, k == c // 64 * 16 + c % 32 // 2)
    k, c = iota((128, 1024), 0), iota((128, 1024), 1)
    put(m_four, k == c // 128 * 16 + c % 32 // 4)

    for copy in deep_k:
        copy.wait_recv()
    for copy in deep_k:
        copy.wait_send()

    @pl.when(mx == 0)
    def _():
        k_fr[:, 0:24] = jnp.zeros((18, 24, 128), F32)

    @pl.when(mx == N_X - 1)
    def _():
        k_fr[:, 56:80] = jnp.zeros((18, 24, 128), F32)

    @pl.when(my == 0)
    def _():
        k_fr[0:5] = jnp.zeros((5, 80, 128), F32)

    @pl.when(my == N_Y - 1)
    def _():
        k_fr[13:18] = jnp.zeros((5, 80, 128), F32)

    window = pl.ds(8, 64)

    def coarse_weights(i, carry):
        j = i + 1
        k = k_fr[j, window]
        kxm = k_fr[j, pl.ds(7, 64)]
        kxp = k_fr[j, pl.ds(9, 64)]
        kym = y_before(k_fr, j, window, lanes, 32)
        kyp = y_beyond(k_fr, j, window, lanes, 32)
        kzm = jnp.where(z_first, 0.0, roll(k, 1))
        kzp = jnp.where(z_last, 0.0, roll(k, 127))
        wx[j, window] = 0.5 * (k + kxm)
        wy[j, window] = 0.5 * (k + kym)
        wz[j, window] = jnp.where(z_first, 0.0, 0.5 * (k + kzm))
        inverse = 1.0 / (3.0 * k + 0.5 * (kxm + kxp + kym + kyp + kzm + kzp))
        inverse = jnp.where(k > 0.0, inverse, 0.0)
        inv_a[j, window] = jnp.where(first_c, inverse, 0.0)
        inv_b[j, window] = jnp.where(first_c, 0.0, inverse)
        return carry

    lax.fori_loop(0, 16, coarse_weights, 0)
    w_c = (wx, wy, wz)

    def coarsened(ref):
        stacked = []
        for b in range(4):
            parts = [
                ref[1 + 4 * b + q, pl.ds(8, 32, stride=2)]
                + ref[1 + 4 * b + q, pl.ds(9, 32, stride=2)]
                for q in range(4)
            ]
            stacked.append(jnp.concatenate(parts, axis=1))
        return mapped(jnp.concatenate(stacked, axis=0), m_down[...])

    summed = coarsened(k_fr)
    own_b = pl.ds(8, 32)
    for b in range(4):
        b_k[1 + b, own_b] = 0.125 * summed[32 * b : 32 * b + 32]
    zb_first = lanes % 16 == 0
    zb_last = lanes % 16 == 15
    for b in range(4):
        j = b + 1
        k = b_k[j, own_b]
        kxm = b_k[j, pl.ds(7, 32)]
        kxp = b_k[j, pl.ds(9, 32)]
        kym = y_before(b_k, j, own_b, lanes, 16)
        kyp = y_beyond(b_k, j, own_b, lanes, 16)
        kzm = jnp.where(zb_first, 0.0, roll(k, 1))
        kzp = jnp.where(zb_last, 0.0, roll(k, 127))
        b_wx[j, own_b] = 0.5 * (k + kxm)
        b_wy[j, own_b] = 0.5 * (k + kym)
        b_wz[j, own_b] = jnp.where(zb_first, 0.0, 0.5 * (k + kzm))
        inverse = 1.0 / (3.0 * k + 0.5 * (kxm + kxp + kym + kyp + kzm + kzp))
        inverse = jnp.where(k > 0.0, inverse, 0.0)
        b_ia[b] = jnp.where(first_b, inverse, 0.0)
        b_ib[b] = jnp.where(first_b, 0.0, inverse)

    for copy in deep_r:
        copy.wait_recv()
    for copy in deep_r:
        copy.wait_send()

    for copy in gathered:
        copy.wait_recv()
    for ye in (1, 2):
        for sx in range(4):
            boxes[ye, sx] = box_in[jnp.maximum(found[4 * ye + sx], 0)]
    beside = [
        remote(boxes.at[1], boxes.at[3], sem_s3.at[0], sem_r3.at[0], around[2]),
        remote(boxes.at[2], boxes.at[0], sem_s3.at[1], sem_r3.at[1], around[3]),
    ]

    def compose(ye):
        for oz in range(2):
            pair = [sx for sx in range(4) if (sx + ye) % 2 == oz]
            stacked = [boxes[ye, sx, b] for sx in pair for b in range(2)]
            wide = mapped(jnp.concatenate(stacked, axis=0), m_exp[oz])
            for number, sx in enumerate(pair):
                here = jnp.where(found[4 * ye + sx] >= 0, 1.0, 0.0)
                covered = jnp.where(lanes % 32 // 16 == oz, here, 0.0) > 0.5
                rows = pl.ds(8 + 16 * sx, 16)
                for q in range(4):
                    b, t = q // 2, q % 2
                    j = 1 + 4 * ye + q
                    at = 32 * number + 16 * b
                    part = wide[at : at + 16, 128 * t : 128 * t + 128]
                    mixed = jnp.where(covered, part, r_fr[j, rows])
                    r_fr[j, rows] = mixed
                    e_a[j, rows] = mixed * inv_a[j, rows]

    compose(1)
    compose(2)
    for copy in beside:
        copy.wait_recv()
    compose(0)
    compose(3)

    def second(i, carry):
        j = i + 1
        fresh = r_fr[j, window] + coupled(e_a, w_c, j, 8, 64, lanes, 32)
        e_b[j, window] = fresh * inv_b[j, window]
        return carry

    lax.fori_loop(0, 16, second, 0, unroll=2)

    own_c = pl.ds(24, 32)
    for oz in range(2):
        pair = [(0, oz), (1, 1 - oz)]
        stacked = []
        for ox, oy in pair:
            rows = pl.ds(24 + 16 * ox, 16)
            for b in range(2):
                parts = [
                    e_a[5 + 4 * oy + 2 * b + t, rows] + e_b[5 + 4 * oy + 2 * b + t, rows]
                    for t in range(2)
                ]
                stacked.append(jnp.concatenate(parts, axis=1))
        packed = mapped(jnp.concatenate(stacked, axis=0), m_com[oz])
        for number, (ox, oy) in enumerate(pair):
            for b in range(2):
                at = 32 * number + 16 * b
                e_oct[2 * ox + oy, b] = packed[at : at + 16]
    for h in range(N_X):
        e_out[h] = e_oct[octs[h]]
    returned = to_mates(lambda other: e_out.at[other], e_in, sem_s4, sem_r4)
    e_in[mx] = e_out[mx]

    def remaining(i, carry):
        j = i + 1
        left[j, window] = jnp.where(first_c, coupled(e_b, w_c, j, 8, 64, lanes, 32), 0.0)
        return carry

    lax.fori_loop(0, 16, remaining, 0, unroll=2)
    summed = 0.5 * coarsened(left)
    for b in range(4):
        source = summed[32 * b : 32 * b + 32]
        b_fa[b] = source * b_ia[b]
        b_fb[b] = source * b_ib[b]
        b_ua[1 + b, own_b] = source * b_ia[b]
    w_b = (b_wx, b_wy, b_wz)
    for half in range(2 * SWEEPS - 1):
        into, out_of = ((b_ub, b_ua), (b_ua, b_ub))[half % 2]
        fixed, inverse = ((b_fb, b_ib), (b_fa, b_ia))[half % 2]
        for b in range(4):
            into[1 + b, own_b] = fixed[b] + inverse[b] * coupled(
                out_of, w_b, 1 + b, 8, 32, lanes, 16
            )

    for ox in range(2):
        for oy in range(2):
            rows = pl.ds(16 + 8 * ox, 8)
            u_oct[2 * ox + oy] = b_ua[2 + oy, rows] + b_ub[2 + oy, rows]
    for h in range(N_X):
        u_out[h] = u_oct[octs[h]]
    settled = to_mates(lambda other: u_out.at[other], u_in, sem_s5, sem_r5)
    u_in[mx] = u_out[mx]

    def doubled(ref, pieces):
        for b, piece in enumerate(pieces):
            ref[b, pl.ds(0, 16, stride=2)] = piece
            ref[b, pl.ds(1, 16, stride=2)] = piece
        return mapped(jnp.concatenate([ref[0], ref[1]], axis=0), m_up[...])

    wide = doubled(dup, [b_ua[2 + b, pl.ds(16, 16)] + b_ub[2 + b, pl.ds(16, 16)] for b in range(2)])
    for j in range(8):
        b, q = j // 4, j % 4
        part = wide[32 * b : 32 * b + 32, 128 * q : 128 * q + 128]
        total = e_a[5 + j, own_c] + e_b[5 + j, own_c] + part
        out_c[:, 128 * j : 128 * j + 128] = s_fr[1 + j, own_f] + total

    for copy in returned:
        copy.wait_recv()
    got = e_in.at[owner_x]
    wide = doubled(dup2, [got[0], got[1]])
    for j in range(8):
        b, q = j // 4, j % 4
        f_sm[j] = f_sm[j] + wide[32 * b : 32 * b + 32, 128 * q : 128 * q + 128]
    for copy in settled:
        copy.wait_recv()
    tile = u_in[owner_x]
    side = jnp.where(own_oz == 1, 1.0, 0.0)
    tile = jnp.where(jnp.zeros((8, 128), F32) + side > 0.5, roll(tile, 120), tile)
    for t in range(4):
        dup[0, pl.ds(t, 8, stride=4)] = tile
    wide = mapped(dup[0], m_four[...])
    for j in range(8):
        out_f[0, :, 128 * j : 128 * j + 128] = f_sm[j] + wide[:, 128 * j : 128 * j + 128]

    done = [id(copy) for copy in deep_k + deep_r]
    for copy in sends:
        if id(copy) not in done:
            copy.wait_send()


def scratch():
    v = pltpu.VMEM
    shapes = [(10, 48, 128)] * 2 + [(8, 32, 128)]
    shapes += [(8, 32, 128)] + [(10, 48, 128)] * 8 + [(8, 32, 128), (10, 48, 128)]
    shapes += [(8, 32, 128)] * 2
    shapes += [(18, 80, 128)] * 10
    shapes += [(6, 48, 128)] * 4 + [(4, 32, 128)] * 4 + [(6, 48, 128)] * 2
    shapes += [(4, 16, 128), (4, 16, 128), (N_X, 16, 128), (N_X, 16, 128)]
    shapes += [(2, 16, 128), (N_X, 2, 16, 128), (4, 4, 2, 16, 128)]
    shapes += [(4, 2, 16, 128), (N_X, 2, 16, 128), (N_X, 2, 16, 128)]
    shapes += [(4, 8, 128), (N_X, 8, 128), (N_X, 8, 128)]
    shapes += [(2, 32, 128)] * 2
    result = [v(shape, F32) for shape in shapes]
    maps = [(2, 896, 128), (128, 1280), (512, 128), (128, 512), (2, 128, 256), (2, 256, 128)]
    result += [v(shape, BF16) for shape in maps + [(128, 1024)]]
    dma = pltpu.SemaphoreType.DMA
    result += [dma((7, 8))] + [dma((8,))] * 6 + [dma((N_X,))] * 4 + [dma((2,))] * 2
    return result + [dma((N_X,))] * 4


def on_device(
    coarse_source,
    coarse_coefficient,
    coarse_start,
    fine_source,
    fine_coefficient,
    fine_start,
    fine_position,
    first_colour,
):
    smem = pl.BlockSpec(memory_space=pltpu.SMEM)
    vmem = pl.BlockSpec(memory_space=pltpu.VMEM)
    hbm = pl.BlockSpec(memory_space=pl.ANY)
    return pl.pallas_call(
        kernel,
        out_shape=(
            jax.ShapeDtypeStruct(coarse_start.shape, F32),
            jax.ShapeDtypeStruct(fine_start.shape, F32),
        ),
        in_specs=[smem, smem] + [hbm] * 6,
        out_specs=(vmem, vmem),
        scratch_shapes=scratch(),
        compiler_params=pltpu.CompilerParams(
            collective_id=0, has_side_effects=True, vmem_limit_bytes=48 << 20
        ),
    )(
        fine_position,
        first_colour,
        coarse_source,
        coarse_coefficient,
        coarse_start,
        fine_source,
        fine_coefficient,
        fine_start,
    )


def solution(mesh):
    placed = (
        P("gx", "gy"),
        P("gx", "gy"),
        P("gx", "gy"),
        P(("gx", "gy"), None, None),
        P(("gx", "gy"), None, None),
        P(("gx", "gy"), None, None),
        P(),
        P(),
    )
    return jax.shard_map(
        on_device,
        mesh=mesh,
        in_specs=placed,
        out_specs=(P("gx", "gy"), P(("gx", "gy"), None, None)),
        check_vma=False,
    )
```

profile of v0, /device:TPU:1, one launch (start us, length us, event | category | flops | bytes accessed | tf_op | source)
XLA Modules:
  0.0 52.0 jit_solution(5090533894402278727)
XLA Ops:
  0.6 0.0 copy-start
  0.6 0.9 %copy-done = f32[32,1024]{1,0:T(8,128)S(1)} copy-done((f32[32,1024]{1,0:T(8,128)S(1)}, f32[32,1024]{1,0:T(8,128)}, u32[]{:S(2)}) %copy-start) | copy-done | bytes 131096
  1.5 0.0 copy-start.1
  1.5 0.9 %copy-done.1 = f32[32,1024]{1,0:T(8,128)S(1)} copy-done((f32[32,1024]{1,0:T(8,128)S(1)}, f32[32,1024]{1,0:T(8,128)}, u32[]{:S(2)}) %copy-start.1) | copy-done | bytes 131096
  2.4 0.0 copy-start.2
  2.4 0.9 %copy-done.2 = f32[32,1024]{1,0:T(8,128)S(1)} copy-done((f32[32,1024]{1,0:T(8,128)S(1)}, f32[32,1024]{1,0:T(8,128)}, u32[]{:S(2)}) %copy-start.2) | copy-done | bytes 131096
  3.3 0.0 copy-start.3
  3.3 0.9 %copy-done.3 = f32[1,32,1024]{2,1,0:T(8,128)S(1)} copy-done((f32[1,32,1024]{2,1,0:T(8,128)S(1)}, f32[1,32,1024]{2,1,0:T(8,128)}, u32[]{:S(2)}) %copy-start.3) | copy-done | bytes 131096
  4.3 0.0 copy-start.4
  4.3 0.9 %copy-done.4 = f32[1,32,1024]{2,1,0:T(8,128)S(1)} copy-done((f32[1,32,1024]{2,1,0:T(8,128)S(1)}, f32[1,32,1024]{2,1,0:T(8,128)}, u32[]{:S(2)}) %copy-start.4) | copy-done | bytes 131096
  5.2 0.0 copy-start.5
  5.2 0.9 %copy-done.5 = f32[1,32,1024]{2,1,0:T(8,128)S(1)} copy-done((f32[1,32,1024]{2,1,0:T(8,128)S(1)}, f32[1,32,1024]{2,1,0:T(8,128)}, u32[]{:S(2)}) %copy-start.5) | copy-done | bytes 131096
  6.1 0.0 copy-start.6
  6.1 0.7 %copy-done.6 = s32[128]{0:T(128)S(1)} copy-done((s32[128]{0:T(128)S(1)}, s32[128]{0:T(128)}, u32[]{:S(2)}) %copy-start.6) | copy-done | bytes 536
  6.7 0.0 copy-start.7
  6.7 0.7 %copy-done.7 = s32[3]{0:T(128)S(1)} copy-done((s32[3]{0:T(128)S(1)}, s32[3]{0:T(128)}, u32[]{:S(2)}) %copy-start.7) | copy-done | bytes 36
  7.4 43.3 %shard_map.95 = (f32[32,1024]{1,0:T(8,128)S(1)}, f32[1,32,1024]{2,1,0:T(8,128)S(1)}) custom-call(s32[128]{0:T(128)S(1)} %copy-done.6, s32[3]{0:T(128)S(1)} %copy-done.7, f32[32,1024]{1,0:T(8,128)S(1)} %copy-done, f32[32,1024]{1,0:T(8,128)S(1)} %copy-done.1, f32[32,1024]{1,0:T(8,128)S(1)} %copy-done.2, f32[1,32,1024]{2,1,0:T(8,128)S(1)} %copy-done.3, ...), custom_call_target="tpu_custom_call" | custom-call | tf_op jit(solution)/shard_map/pallas_call | solution.py:762
  50.6 0.7 %copy.12 = f32[32,1024]{1,0:T(8,128)} copy(f32[32,1024]{1,0:T(8,128)S(1)} %get-tuple-element.4) | data formatting | bytes 262144
  51.3 0.7 %copy.13 = f32[1,32,1024]{2,1,0:T(8,128)} copy(f32[1,32,1024]{2,1,0:T(8,128)S(1)} %get-tuple-element.5) | data formatting | bytes 262144
Async XLA Ops:
  0.6 0.9 %copy-start = (f32[32,1024]{1,0:T(8,128)S(1)}, f32[32,1024]{1,0:T(8,128)}, u32[]{:S(2)}) copy-start(f32[32,1024]{1,0:T(8,128)} %c_source.1) | copy-start | bytes 393220
  1.5 0.9 %copy-start.1 = (f32[32,1024]{1,0:T(8,128)S(1)}, f32[32,1024]{1,0:T(8,128)}, u32[]{:S(2)}) copy-start(f32[32,1024]{1,0:T(8,128)} %c_coeff.1) | copy-start | bytes 393220
  2.4 0.9 %copy-start.2 = (f32[32,1024]{1,0:T(8,128)S(1)}, f32[32,1024]{1,0:T(8,128)}, u32[]{:S(2)}) copy-start(f32[32,1024]{1,0:T(8,128)} %c_start.1) | copy-start | bytes 393220
  3.3 0.9 %copy-start.3 = (f32[1,32,1024]{2,1,0:T(8,128)S(1)}, f32[1,32,1024]{2,1,0:T(8,128)}, u32[]{:S(2)}) copy-start(f32[1,32,1024]{2,1,0:T(8,128)} %f_source.1) | copy-start | bytes 393220
  4.3 0.9 %copy-start.4 = (f32[1,32,1024]{2,1,0:T(8,128)S(1)}, f32[1,32,1024]{2,1,0:T(8,128)}, u32[]{:S(2)}) copy-start(f32[1,32,1024]{2,1,0:T(8,128)} %f_coeff.1) | copy-start | bytes 393220
  5.2 0.9 %copy-start.5 = (f32[1,32,1024]{2,1,0:T(8,128)S(1)}, f32[1,32,1024]{2,1,0:T(8,128)}, u32[]{:S(2)}) copy-start(f32[1,32,1024]{2,1,0:T(8,128)} %f_start.1) | copy-start | bytes 393220
  6.1 0.7 %copy-start.6 = (s32[128]{0:T(128)S(1)}, s32[128]{0:T(128)}, u32[]{:S(2)}) copy-start(s32[128]{0:T(128)} %pos.1) | copy-start | bytes 1540
  6.7 0.7 %copy-start.7 = (s32[3]{0:T(128)S(1)}, s32[3]{0:T(128)}, u32[]{:S(2)}) copy-start(s32[3]{0:T(128)} %colours.1) | copy-start | bytes 40
where the time goes:
time: 52.2 us; the launch traced here: 52 us
  Pallas kernels  43.3 us (83%)
  local copies, waits for them, and re-layouts  8.04 us (15%)
  between operations  0.66 us (1%)
    pallas_call x1, Pallas kernels, on_device(): pl.pallas_call(kernel, out_shape=(jax.ShapeDtypeStruct(coarse_start.shape...  43.3 us
    unnamed x18, local copies, waits for them, and re-layouts  8.04 us

commit v1 on v0

--- a/solution.py
+++ b/solution.py
@@ -65,6 +65,24 @@
     ref[blocks - 1] = jnp.zeros((rows, 128), F32)
     ref[1 : blocks - 1, :low] = jnp.zeros((blocks - 2, low, 128), F32)
     ref[1 : blocks - 1, high:] = jnp.zeros((blocks - 2, rows - high, 128), F32)
+
+
+class Remote:
+    def __init__(self, copy):
+        self.copy = copy
+        self.landed = False
+        self.left = False
+        copy.start()
+
+    def wait_recv(self):
+        if not self.landed:
+            self.copy.wait_recv()
+        self.landed = True
+
+    def wait_send(self):
+        if not self.left:
+            self.copy.wait_send()
+        self.left = True
 
 
 def put(ref, mask):
@@ -167,12 +185,13 @@
         (x_up, my),
         (mx, y_dn),
         (mx, y_up),
-        (x_dn, y_dn),
-        (x_dn, y_up),
-        (x_up, y_dn),
-        (x_up, y_up),
     ]
     mates = [(lax.rem(mx + d, N_X), my) for d in range(1, N_X)]
+
+    for blocks in (pl.ds(0, 5), pl.ds(13, 5)):
+        for rows in (pl.ds(0, 24), pl.ds(56, 24)):
+            k_fr[blocks, rows] = jnp.zeros((5, 24, 128), F32)
+            r_fr[blocks, rows] = jnp.zeros((5, 24, 128), F32)
 
     barrier = pltpu.get_barrier_semaphore()
     greeted = mates + around[2:]
@@ -269,15 +288,16 @@
     sends = []
 
     def remote(source, target, send_sem, recv_sem, device):
-        copy = pltpu.make_async_remote_copy(
-            src_ref=source,
-            dst_ref=target,
-            send_sem=send_sem,
-            recv_sem=recv_sem,
-            device_id=device,
-            device_id_type=MESH,
+        copy = Remote(
+            pltpu.make_async_remote_copy(
+                src_ref=source,
+                dst_ref=target,
+                send_sem=send_sem,
+                recv_sem=recv_sem,
+                device_id=device,
+                device_id_type=MESH,
+            )
         )
-        copy.start()
         sends.append(copy)
         return copy
 
@@ -294,6 +314,43 @@
         ):
             at = 4 * number + side
             layer.append(remote(source, target, sem_s0.at[at], sem_r0.at[at], device))
+
+    for copy in loads[6]:
+        copy.wait()
+
+    def deep_x(ref, width, send_sem, recv_sem):
+        blocks = pl.ds(5, 8)
+        started = []
+        for side, (source, target) in enumerate(((24, 56), (56 - width, 24 - width))):
+            started.append(
+                remote(
+                    ref.at[blocks, pl.ds(source, width)],
+                    ref.at[blocks, pl.ds(target, width)],
+                    send_sem.at[side],
+                    recv_sem.at[side],
+                    around[side],
+                )
+            )
+        return started
+
+    def deep_y(ref, depth, send_sem, recv_sem):
+        started = []
+        for q in range(depth):
+            rows = pl.ds(8 + 4 * q, 64 - 8 * q)
+            for side, (source, target) in enumerate(((5 + q, 13 + q), (12 - q, 4 - q))):
+                at = 2 + 2 * q + side
+                started.append(
+                    remote(
+                        ref.at[source, rows],
+                        ref.at[target, rows],
+                        send_sem.at[at],
+                        recv_sem.at[at],
+                        around[2 + side],
+                    )
+                )
+        return started
+
+    deep_k = deep_x(k_fr, 17, sem_sk, sem_rk)
 
     for group in loads[2:5]:
         for copy in group:
@@ -379,41 +436,6 @@
     ghosts = to_mates(lambda other: ghost_out.at[other], ghost_in, sem_s1, sem_r1)
     ghost_in[mx] = ghost_out[mx]
 
-    for copy in loads[6]:
-        copy.wait()
-
-    def deep(ref, base, width, blocks, send_sem, recv_sem):
-        full_r, full_b = (base, base, 32), (5, 5, 8)
-        r_low = (base, base + 32, width)
-        r_high = (base + 32 - width, base - width, width)
-        b_low = (5, 13, blocks)
-        b_high = (13 - blocks, 5 - blocks, blocks)
-        started = []
-        for number, (r, b) in enumerate(
-            (
-                (r_low, full_b),
-                (r_high, full_b),
-                (full_r, b_low),
-                (full_r, b_high),
-                (r_low, b_low),
-                (r_low, b_high),
-                (r_high, b_low),
-                (r_high, b_high),
-            )
-        ):
-            started.append(
-                remote(
-                    ref.at[pl.ds(b[0], b[2]), pl.ds(r[0], r[2])],
-                    ref.at[pl.ds(b[1], b[2]), pl.ds(r[1], r[2])],
-                    send_sem.at[number],
-                    recv_sem.at[number],
-                    around[number],
-                )
-            )
-        return started
-
-    deep_k = deep(k_fr, 24, 24, 5, sem_sk, sem_rk)
-
     for copy in loads[5]:
         copy.wait()
 
@@ -443,7 +465,20 @@
         return carry
 
     lax.fori_loop(0, 8, coarse_residual, 0)
-    deep_r = deep(r_fr, 24, 16, 4, sem_sr, sem_rr)
+    deep_r = deep_x(r_fr, 16, sem_sr, sem_rr)
+
+    for copy in deep_k:
+        copy.wait_recv()
+
+    @pl.when(mx == 0)
+    def _():
+        k_fr[5:13, 7:24] = jnp.zeros((8, 17, 128), F32)
+
+    @pl.when(mx == N_X - 1)
+    def _():
+        k_fr[5:13, 56:73] = jnp.zeros((8, 17, 128), F32)
+
+    deep_k += deep_y(k_fr, 5, sem_sk, sem_rk)
 
     k = iota((128, 1280), 0)
     c = iota((128, 1280), 1)
@@ -494,6 +529,9 @@
     box_out[1] = packed[16:]
     gathered = to_mates(lambda other: box_out, box_in, sem_s2, sem_r2)
     box_in[mx] = box_out[...]
+    for copy in deep_r:
+        copy.wait_recv()
+    deep_r += deep_y(r_fr, 4, sem_sr, sem_rr)
 
     zero_pads(wx, 8, 72)
     zero_pads(wy, 8, 72)
@@ -513,17 +551,6 @@
 
     for copy in deep_k:
         copy.wait_recv()
-    for copy in deep_k:
-        copy.wait_send()
-
-    @pl.when(mx == 0)
-    def _():
-        k_fr[:, 0:24] = jnp.zeros((18, 24, 128), F32)
-
-    @pl.when(mx == N_X - 1)
-    def _():
-        k_fr[:, 56:80] = jnp.zeros((18, 24, 128), F32)
-
     @pl.when(my == 0)
     def _():
         k_fr[0:5] = jnp.zeros((5, 80, 128), F32)
@@ -720,10 +747,8 @@
     for j in range(8):
         out_f[0, :, 128 * j : 128 * j + 128] = f_sm[j] + wide[:, 128 * j : 128 * j + 128]
 
-    done = [id(copy) for copy in deep_k + deep_r]
     for copy in sends:
-        if id(copy) not in done:
-            copy.wait_send()
+        copy.wait_send()
 
 
 def scratch():
@@ -742,7 +767,7 @@
     maps = [(2, 896, 128), (128, 1280), (512, 128), (128, 512), (2, 128, 256), (2, 256, 128)]
     result += [v(shape, BF16) for shape in maps + [(128, 1024)]]
     dma = pltpu.SemaphoreType.DMA
-    result += [dma((7, 8))] + [dma((8,))] * 6 + [dma((N_X,))] * 4 + [dma((2,))] * 2
+    result += [dma((7, 8))] + [dma((8,))] * 2 + [dma((12,))] * 4 + [dma((N_X,))] * 4 + [dma((2,))] * 2
     return result + [dma((N_X,))] * 4
 
 
@@ -758,7 +783,7 @@
 ):
     smem = pl.BlockSpec(memory_space=pltpu.SMEM)
     vmem = pl.BlockSpec(memory_space=pltpu.VMEM)
-    hbm = pl.BlockSpec(memory_space=pl.ANY)
+    hbm = pl.BlockSpec(memory_space=pltpu.HBM)
     return pl.pallas_call(
         kernel,
         out_shape=(
@@ -772,14 +797,19 @@
             collective_id=0, has_side_effects=True, vmem_limit_bytes=48 << 20
         ),
     )(
-        fine_position,
-        first_colour,
-        coarse_source,
-        coarse_coefficient,
-        coarse_start,
-        fine_source,
-        fine_coefficient,
-        fine_start,
+        *[
+            pltpu.with_memory_space_constraint(array, pltpu.HBM)
+            for array in (
+                fine_position,
+                first_colour,
+                coarse_source,
+                coarse_coefficient,
+                coarse_start,
+                fine_source,
+                fine_coefficient,
+                fine_start,
+            )
+        ],
     )
 
 

time: 52.2 us -> 39.8 us (0.76)
  local copies, waits for them, and re-layouts: 8.04 us -> 1.31 us
  Pallas kernels: 43.3 us -> 37.7 us
    unnamed x18 -> x2, local copies, waits for them, and re-layouts: 8.04 us -> 1.31 us
    pallas_call x1, Pallas kernels: 43.3 us -> 37.7 us  [on_device(): pl.pallas_call(kernel, out_shape=(jax.ShapeDtypeStruct(coarse_start.shape...]
where the time goes in v1:
time: 39.8 us; the launch traced here: 39.6 us
  Pallas kernels  37.7 us (95%)
  local copies, waits for them, and re-layouts  1.31 us (3%)
  between operations  0.64 us (2%)
    pallas_call x1, Pallas kernels, on_device(): pl.pallas_call(kernel, out_shape=(jax.ShapeDtypeStruct(coarse_start.shape...  37.7 us
    unnamed x2, local copies, waits for them, and re-layouts  1.31 us

profile of v1, /device:TPU:1, one launch (start us, length us, event | category | flops | bytes accessed | tf_op | source)
XLA Modules:
  0.0 39.6 jit_solution(703387220867519109)
XLA Ops:
  0.6 37.7 %shard_map.95 = (f32[32,1024]{1,0:T(8,128)S(1)}, f32[1,32,1024]{2,1,0:T(8,128)S(1)}) custom-call(s32[128]{0:T(128)} %pos.1, s32[3]{0:T(128)} %colours.1, f32[32,1024]{1,0:T(8,128)} %c_source.1, f32[32,1024]{1,0:T(8,128)} %c_coeff.1, f32[32,1024]{1,0:T(8,128)} %c_start.1, f32[1,32,1024]{2,1,0:T(8,128)} %f_source.1, f32[1,32,1024]{2,1,0:T(8,128)} %f_coeff.1, ...), custom_call_target="tpu_custom_call" | custom-call | tf_op jit(solution)/shard_map/pallas_call | solution.py:787
  38.3 0.7 %copy.12 = f32[32,1024]{1,0:T(8,128)} copy(f32[32,1024]{1,0:T(8,128)S(1)} %get-tuple-element.4) | data formatting | bytes 262144
  39.0 0.7 %copy.13 = f32[1,32,1024]{2,1,0:T(8,128)} copy(f32[1,32,1024]{2,1,0:T(8,128)S(1)} %get-tuple-element.5) | data formatting | bytes 262144

commit v2 on v1

--- a/solution.py
+++ b/solution.py
@@ -90,8 +90,8 @@
 
 
 def kernel(
-    pos,
-    colours,
+    pos_hbm,
+    colours_hbm,
     c_source,
     c_coeff,
     c_start,
@@ -100,6 +100,8 @@
     f_start,
     out_c,
     out_f,
+    pos,
+    colours,
     s_fr,
     kq_fr,
     src_c,
@@ -188,17 +190,19 @@
     ]
     mates = [(lax.rem(mx + d, N_X), my) for d in range(1, N_X)]
 
-    for blocks in (pl.ds(0, 5), pl.ds(13, 5)):
-        for rows in (pl.ds(0, 24), pl.ds(56, 24)):
-            k_fr[blocks, rows] = jnp.zeros((5, 24, 128), F32)
-            r_fr[blocks, rows] = jnp.zeros((5, 24, 128), F32)
-
     barrier = pltpu.get_barrier_semaphore()
     greeted = mates + around[2:]
     for device in greeted:
         pl.semaphore_signal(barrier, inc=1, device_id=device, device_id_type=MESH)
 
-    loads = []
+    loads = [
+        [
+            pltpu.make_async_copy(pos_hbm, pos, sem_l.at[7, 0]),
+            pltpu.make_async_copy(colours_hbm, colours, sem_l.at[7, 1]),
+        ]
+    ]
+    for copy in loads[0]:
+        copy.start()
 
     def load(number, source, target):
         group = []
@@ -219,6 +223,13 @@
     load(5, lambda j: c_source.at[:, chunk(j)], lambda j: src_c.at[j])
     load(6, lambda j: c_coeff.at[:, chunk(j)], lambda j: k_fr.at[5 + j, pl.ds(24, 32)])
 
+    for q in range(5):
+        for j in (4 - q, 13 + q):
+            for low, high in ((0, 8 + 4 * q), (72 - 4 * q, 80)):
+                k_fr[j, low:high] = jnp.zeros((high - low, 128), F32)
+                r_fr[j, low:high] = jnp.zeros((high - low, 128), F32)
+    for copy in loads[0]:
+        copy.wait()
     own_pos = pos[mx * N_Y + my]
     owner_x = own_pos >> 6
     own_oz = own_pos & 1
@@ -242,7 +253,14 @@
         return tuple(result)
 
     found = lax.fori_loop(0, N_X, look, tuple(jnp.int32(-1) for _ in slots))
-    octs = [(pos[h * N_Y + my] >> 1) & 3 for h in range(N_X)]
+    octs, picks = [], []
+    for h in range(N_X):
+        at = pos[h * N_Y + my]
+        octant, away = (at >> 1) & 3, (at >> 6) - mx
+        pick = jnp.where((away == 1) & (octant < 2), 4 + octant, 0)
+        pick = jnp.where((away == -1) & (octant >= 2), 4 + octant, pick)
+        octs.append(octant)
+        picks.append(jnp.where(away == 0, octant, pick))
 
     lanes = iota((1, 128), 1)
     z_first = lanes % 32 == 0
@@ -280,9 +298,34 @@
         )
         m_face[oz] = jnp.where(mask, 1.0, 0.0).astype(BF16)
 
-    for group in loads[:2]:
+    for group in loads[1:3]:
         for copy in group:
             copy.wait()
+
+    for ox in range(2):
+        for oy in range(2):
+            own, at = (24, 4) if ox == 0 else (23, 0)
+            far, at_far = (39, 0) if ox == 0 else (8, 4)
+            for q in range(4):
+                j = 1 + 4 * oy + q
+                x_rows[2 * ox + oy, at + q : at + q + 1] = s_fr[j, own : own + 1]
+                x_rows[4 + 2 * ox + oy, at_far + q : at_far + q + 1] = s_fr[j, far : far + 1]
+    blank = jnp.zeros((16, 128), F32)
+    for oz in range(2):
+        pair = [(0, oz), (1, 1 - oz)]
+        stacked = []
+        for ox, oy in pair:
+            rows = pl.ds(8 + 16 * ox, 16)
+            parts = [s_fr[4, rows], blank] if oy else [blank, s_fr[5, rows]]
+            parts += [s_fr[1 + 4 * oy + q, rows] for q in range(4)]
+            parts.append(x_rows[2 * ox + oy])
+            stacked.append(jnp.concatenate(parts, axis=1))
+        for ox, oy in pair:
+            stacked.append(jnp.concatenate([blank] * 6 + [x_rows[4 + 2 * ox + oy]], axis=1))
+        packed = mapped(jnp.concatenate(stacked, axis=0), m_face[oz])
+        for number, (ox, oy) in enumerate(pair):
+            faces[2 * ox + oy] = packed[16 * number : 16 * number + 16]
+            faces[4 + 2 * ox + oy] = packed[32 + 16 * number : 48 + 16 * number]
     pl.semaphore_wait(barrier, len(greeted))
 
     sends = []
@@ -315,7 +358,7 @@
             at = 4 * number + side
             layer.append(remote(source, target, sem_s0.at[at], sem_r0.at[at], device))
 
-    for copy in loads[6]:
+    for copy in loads[7]:
         copy.wait()
 
     def deep_x(ref, width, send_sem, recv_sem):
@@ -352,7 +395,7 @@
 
     deep_k = deep_x(k_fr, 17, sem_sk, sem_rk)
 
-    for group in loads[2:5]:
+    for group in loads[3:6]:
         for copy in group:
             copy.wait()
     rows_f = iota((32, 128), 0)
@@ -384,18 +427,10 @@
 
     lax.fori_loop(0, 8, fine_base, 0)
 
-    for copy in layer:
-        copy.wait_recv()
-    for ref in (s_fr, kq_fr):
-
-        @pl.when(mx == 0)
-        def _():
-            ref[1:9, 7:8] = jnp.zeros((8, 1, 128), F32)
-
-        @pl.when(mx == N_X - 1)
-        def _():
-            ref[1:9, 40:41] = jnp.zeros((8, 1, 128), F32)
-
+    for copy in layer[:2]:
+        copy.wait_recv()
+
+    def blank_sides(ref):
         @pl.when(my == 0)
         def _():
             ref[0, 8:40] = jnp.zeros((32, 128), F32)
@@ -404,23 +439,18 @@
         def _():
             ref[9, 8:40] = jnp.zeros((32, 128), F32)
 
+    blank_sides(s_fr)
+
     for ox in range(2):
         for oy in range(2):
-            for q in range(4):
-                for at, row in ((q, 7 + 16 * ox), (4 + q, 24 + 16 * ox)):
-                    x_rows[2 * ox + oy, at : at + 1] = s_fr[1 + 4 * oy + q, row : row + 1]
-    for oz in range(2):
-        pair = [(0, oz), (1, 1 - oz)]
-        stacked = []
-        for ox, oy in pair:
             rows = pl.ds(8 + 16 * ox, 16)
-            parts = [s_fr[4 * oy, rows], s_fr[5 + 4 * oy, rows]]
-            parts += [s_fr[1 + 4 * oy + q, rows] for q in range(4)]
-            parts.append(x_rows[2 * ox + oy])
-            stacked.append(jnp.concatenate(parts, axis=1))
-        packed = mapped(jnp.concatenate(stacked, axis=0), m_face[oz])
-        for number, (ox, oy) in enumerate(pair):
-            faces[2 * ox + oy] = packed[16 * number : 16 * number + 16]
+            oz = (ox + oy) % 2
+            shift = (128 - 96 - 16 * oz, 16 - 16 * oz)[oy] % 128
+            beside = s_fr[9 * oy, rows]
+            if shift:
+                beside = roll(beside, shift)
+            wanted = (lanes >= 16 * oy) & (lanes < 16 * oy + 16)
+            faces[2 * ox + oy] = faces[2 * ox + oy] + jnp.where(wanted, beside, 0.0)
 
     def to_mates(source, target, send_sem, recv_sem):
         started = []
@@ -432,11 +462,24 @@
         return started
 
     for h in range(N_X):
-        ghost_out[h] = faces[octs[h]]
+        ghost_out[h] = faces[picks[h]]
     ghosts = to_mates(lambda other: ghost_out.at[other], ghost_in, sem_s1, sem_r1)
     ghost_in[mx] = ghost_out[mx]
 
-    for copy in loads[5]:
+    for copy in layer:
+        copy.wait_recv()
+    blank_sides(kq_fr)
+    for ref in (s_fr, kq_fr):
+
+        @pl.when(mx == 0)
+        def _():
+            ref[1:9, 7:8] = jnp.zeros((8, 1, 128), F32)
+
+        @pl.when(mx == N_X - 1)
+        def _():
+            ref[1:9, 40:41] = jnp.zeros((8, 1, 128), F32)
+
+    for copy in loads[6]:
         copy.wait()
 
     def coarse_residual(i, carry):
@@ -495,7 +538,11 @@
 
     for copy in ghosts:
         copy.wait_recv()
-    mine = ghost_in[owner_x]
+    high_x = (own_pos >> 2) & 1
+    other_x = owner_x + 2 * high_x - 1
+    beyond_x = ghost_in[jnp.clip(other_x, 0, N_X - 1)]
+    inside = jnp.where((other_x >= 0) & (other_x < N_X), 1.0, 0.0)
+    mine = ghost_in[owner_x] + inside * beyond_x
     dup[0, pl.ds(0, 16, stride=2)] = mine
     dup[0, pl.ds(1, 16, stride=2)] = mine
     widened = mapped(dup[0], m_ghost[...])
@@ -753,21 +800,22 @@
 
 def scratch():
     v = pltpu.VMEM
+    lists = [pltpu.SMEM((N_X * N_Y,), jnp.int32), pltpu.SMEM((3,), jnp.int32)]
     shapes = [(10, 48, 128)] * 2 + [(8, 32, 128)]
     shapes += [(8, 32, 128)] + [(10, 48, 128)] * 8 + [(8, 32, 128), (10, 48, 128)]
     shapes += [(8, 32, 128)] * 2
     shapes += [(18, 80, 128)] * 10
     shapes += [(6, 48, 128)] * 4 + [(4, 32, 128)] * 4 + [(6, 48, 128)] * 2
-    shapes += [(4, 16, 128), (4, 16, 128), (N_X, 16, 128), (N_X, 16, 128)]
+    shapes += [(8, 16, 128), (8, 16, 128), (N_X, 16, 128), (N_X, 16, 128)]
     shapes += [(2, 16, 128), (N_X, 2, 16, 128), (4, 4, 2, 16, 128)]
     shapes += [(4, 2, 16, 128), (N_X, 2, 16, 128), (N_X, 2, 16, 128)]
     shapes += [(4, 8, 128), (N_X, 8, 128), (N_X, 8, 128)]
     shapes += [(2, 32, 128)] * 2
-    result = [v(shape, F32) for shape in shapes]
+    result = lists + [v(shape, F32) for shape in shapes]
     maps = [(2, 896, 128), (128, 1280), (512, 128), (128, 512), (2, 128, 256), (2, 256, 128)]
     result += [v(shape, BF16) for shape in maps + [(128, 1024)]]
     dma = pltpu.SemaphoreType.DMA
-    result += [dma((7, 8))] + [dma((8,))] * 2 + [dma((12,))] * 4 + [dma((N_X,))] * 4 + [dma((2,))] * 2
+    result += [dma((8, 8))] + [dma((8,))] * 2 + [dma((12,))] * 4 + [dma((N_X,))] * 4 + [dma((2,))] * 2
     return result + [dma((N_X,))] * 4
 
 
@@ -781,7 +829,6 @@
     fine_position,
     first_colour,
 ):
-    smem = pl.BlockSpec(memory_space=pltpu.SMEM)
     vmem = pl.BlockSpec(memory_space=pltpu.VMEM)
     hbm = pl.BlockSpec(memory_space=pltpu.HBM)
     return pl.pallas_call(
@@ -790,7 +837,7 @@
             jax.ShapeDtypeStruct(coarse_start.shape, F32),
             jax.ShapeDtypeStruct(fine_start.shape, F32),
         ),
-        in_specs=[smem, smem] + [hbm] * 6,
+        in_specs=[hbm] * 8,
         out_specs=(vmem, vmem),
         scratch_shapes=scratch(),
         compiler_params=pltpu.CompilerParams(

time: 39.8 us -> 37.5 us (0.942)
  the two profiles are of different devices: /device:TPU:1 before, /device:TPU:0 now
where the time goes in v2:
time: 37.5 us; the launch traced here: 37.3 us
  Pallas kernels  35.4 us (94%)
  local copies, waits for them, and re-layouts  1.31 us (3%)
  between operations  0.64 us (2%)
    pallas_call x1, Pallas kernels, on_device(): pl.pallas_call(kernel, out_shape=(jax.ShapeDtypeStruct(coarse_start.shape...  35.4 us
    unnamed x2, local copies, waits for them, and re-layouts  1.31 us

profile of v2, /device:TPU:0, one launch (start us, length us, event | category | flops | bytes accessed | tf_op | source)
XLA Modules:
  0.0 37.3 jit_solution(16333288668968771549)
XLA Ops:
  0.6 35.4 %shard_map.95 = (f32[32,1024]{1,0:T(8,128)S(1)}, f32[1,32,1024]{2,1,0:T(8,128)S(1)}) custom-call(s32[128]{0:T(128)} %pos_hbm.1, s32[3]{0:T(128)} %colours_hbm.1, f32[32,1024]{1,0:T(8,128)} %c_source.1, f32[32,1024]{1,0:T(8,128)} %c_coeff.1, f32[32,1024]{1,0:T(8,128)} %c_start.1, f32[1,32,1024]{2,1,0:T(8,128)} %f_source.1, f32[1,32,1024]{2,1,0:T(8,128)} %f_coeff.1, ...), custom_call_target="tpu_custom_call" | custom-call | tf_op jit(solution)/shard_map/pallas_call | solution.py:834
  36.0 0.7 %copy.12 = f32[32,1024]{1,0:T(8,128)} copy(f32[32,1024]{1,0:T(8,128)S(1)} %get-tuple-element.4) | data formatting | bytes 262144
  36.7 0.7 %copy.13 = f32[1,32,1024]{2,1,0:T(8,128)} copy(f32[1,32,1024]{2,1,0:T(8,128)S(1)} %get-tuple-element.5) | data formatting | bytes 262144

commit v3 on v2

--- a/solution.py
+++ b/solution.py
@@ -14,6 +14,8 @@
 SWEEPS = 4
 N_X = 16
 N_Y = 8
+FAR_FIRST = (10, 6, 9, 11, 7, 5, 14, 2, 8, 13, 15, 3, 1, 12, 4)
+UNROLL = 16
 
 
 def iota(shape, dim):
@@ -98,8 +100,7 @@
     f_source,
     f_coeff,
     f_start,
-    out_c,
-    out_f,
+    out,
     pos,
     colours,
     s_fr,
@@ -188,7 +189,7 @@
         (mx, y_dn),
         (mx, y_up),
     ]
-    mates = [(lax.rem(mx + d, N_X), my) for d in range(1, N_X)]
+    mates = [(lax.rem(mx + d, N_X), my) for d in FAR_FIRST]
 
     barrier = pltpu.get_barrier_semaphore()
     greeted = mates + around[2:]
@@ -454,7 +455,7 @@
 
     def to_mates(source, target, send_sem, recv_sem):
         started = []
-        for d in range(1, N_X):
+        for d in FAR_FIRST:
             other = lax.rem(mx + d, N_X)
             started.append(
                 remote(source(other), target.at[mx], send_sem.at[d], recv_sem.at[d], (other, my))
@@ -709,7 +710,7 @@
         e_b[j, window] = fresh * inv_b[j, window]
         return carry
 
-    lax.fori_loop(0, 16, second, 0, unroll=2)
+    lax.fori_loop(0, 16, second, 0, unroll=UNROLL)
 
     own_c = pl.ds(24, 32)
     for oz in range(2):
@@ -738,7 +739,7 @@
         left[j, window] = jnp.where(first_c, coupled(e_b, w_c, j, 8, 64, lanes, 32), 0.0)
         return carry
 
-    lax.fori_loop(0, 16, remaining, 0, unroll=2)
+    lax.fori_loop(0, 16, remaining, 0, unroll=UNROLL)
     summed = 0.5 * coarsened(left)
     for b in range(4):
         source = summed[32 * b : 32 * b + 32]
@@ -774,7 +775,7 @@
         b, q = j // 4, j % 4
         part = wide[32 * b : 32 * b + 32, 128 * q : 128 * q + 128]
         total = e_a[5 + j, own_c] + e_b[5 + j, own_c] + part
-        out_c[:, 128 * j : 128 * j + 128] = s_fr[1 + j, own_f] + total
+        out[0, :, 128 * j : 128 * j + 128] = s_fr[1 + j, own_f] + total
 
     for copy in returned:
         copy.wait_recv()
@@ -792,7 +793,7 @@
         dup[0, pl.ds(t, 8, stride=4)] = tile
     wide = mapped(dup[0], m_four[...])
     for j in range(8):
-        out_f[0, :, 128 * j : 128 * j + 128] = f_sm[j] + wide[:, 128 * j : 128 * j + 128]
+        out[1, :, 128 * j : 128 * j + 128] = f_sm[j] + wide[:, 128 * j : 128 * j + 128]
 
     for copy in sends:
         copy.wait_send()
@@ -831,14 +832,11 @@
 ):
     vmem = pl.BlockSpec(memory_space=pltpu.VMEM)
     hbm = pl.BlockSpec(memory_space=pltpu.HBM)
-    return pl.pallas_call(
+    both = pl.pallas_call(
         kernel,
-        out_shape=(
-            jax.ShapeDtypeStruct(coarse_start.shape, F32),
-            jax.ShapeDtypeStruct(fine_start.shape, F32),
-        ),
+        out_shape=jax.ShapeDtypeStruct((2, 32, 1024), F32),
         in_specs=[hbm] * 8,
-        out_specs=(vmem, vmem),
+        out_specs=vmem,
         scratch_shapes=scratch(),
         compiler_params=pltpu.CompilerParams(
             collective_id=0, has_side_effects=True, vmem_limit_bytes=48 << 20
@@ -858,6 +856,7 @@
             )
         ],
     )
+    return both[0], both[1:]
 
 
 def solution(mesh):

time: 37.5 us -> 35.4 us (0.944)
  Pallas kernels: 35.4 us -> 33.9 us
  local copies, waits for them, and re-layouts: 1.31 us -> 0.72 us
    pallas_call x1, Pallas kernels: 35.4 us -> 33.9 us  [on_device(): pl.pallas_call(kernel, out_shape=jax.ShapeDtypeStruct((2, 32, 1024), F32)...]
    unnamed x2 -> x0, local copies, waits for them, and re-layouts: 1.31 us -> none
    slice x0 -> x1, local copies, waits for them, and re-layouts: none -> 0.72 us  [on_device(): return (both[0], both[1:])]
where the time goes in v3:
time: 35.4 us; the launch traced here: 35.3 us
  Pallas kernels  33.9 us (96%)
  local copies, waits for them, and re-layouts  0.72 us (2%)
  between operations  0.64 us (2%)
    pallas_call x1, Pallas kernels, on_device(): pl.pallas_call(kernel, out_shape=jax.ShapeDtypeStruct((2, 32, 1024), F32)...  33.9 us
    slice x1, local copies, waits for them, and re-layouts, on_device(): return (both[0], both[1:])  0.72 us

profile of v3, /device:TPU:0, one launch (start us, length us, event | category | flops | bytes accessed | tf_op | source)
XLA Modules:
  0.0 35.3 jit_solution(7090914464072467583)
XLA Ops:
  0.6 33.9 %shard_map.95 = f32[2,32,1024]{2,1,0:T(8,128)S(1)} custom-call(s32[128]{0:T(128)} %pos_hbm.1, s32[3]{0:T(128)} %colours_hbm.1, f32[32,1024]{1,0:T(8,128)} %c_source.1, f32[32,1024]{1,0:T(8,128)} %c_coeff.1, f32[32,1024]{1,0:T(8,128)} %c_start.1, f32[1,32,1024]{2,1,0:T(8,128)} %f_source.1, f32[1,32,1024]{2,1,0:T(8,128)} %f_coeff.1, f32[1,32,1024]{2,1,0:T(8,128)} %f_start.1), custom_call_target="tpu_custom_call" | custom-call | tf_op jit(solution)/shard_map/pallas_call | solution.py:835
  34.6 0.7 %fusion = (f32[1,32,1024]{2,1,0:T(8,128)}, f32[32,1024]{1,0:T(8,128)}) fusion(f32[2,32,1024]{2,1,0:T(8,128)S(1)} %shard_map.95), kind=kLoop, calls=%fused_computation.1 | loop fusion | bytes 524288 | tf_op jit(solution)/shard_map/slice | solution.py:859

commit v4 on v3

--- a/solution.py
+++ b/solution.py
@@ -85,6 +85,18 @@
         if not self.left:
             self.copy.wait_send()
         self.left = True
+
+
+class Group:
+    def __init__(self, span, send_sem, recv_sem):
+        self.sent = pltpu.make_async_copy(span, span, send_sem)
+        self.landed = pltpu.make_async_copy(span, span, recv_sem)
+
+    def wait_recv(self):
+        self.landed.wait()
+
+    def wait_send(self):
+        self.sent.wait()
 
 
 def put(ref, mask):
@@ -198,31 +210,28 @@
 
     loads = [
         [
-            pltpu.make_async_copy(pos_hbm, pos, sem_l.at[7, 0]),
-            pltpu.make_async_copy(colours_hbm, colours, sem_l.at[7, 1]),
+            pltpu.make_async_copy(pos_hbm, pos, sem_l.at[7]),
+            pltpu.make_async_copy(colours_hbm, colours, sem_l.at[8]),
         ]
     ]
     for copy in loads[0]:
         copy.start()
 
-    def load(number, source, target):
-        group = []
+    def load(number, source, target, span):
         for j in range(8):
-            copy = pltpu.make_async_copy(source(j), target(j), sem_l.at[number, j])
-            copy.start()
-            group.append(copy)
-        loads.append(group)
+            pltpu.make_async_copy(source(j), target(j), sem_l.at[number]).start()
+        loads.append([pltpu.make_async_copy(span, span, sem_l.at[number])])
 
     def chunk(j):
         return pl.ds(128 * j, 128)
 
-    load(0, lambda j: c_start.at[:, chunk(j)], lambda j: s_fr.at[1 + j, pl.ds(8, 32)])
-    load(1, lambda j: c_coeff.at[:, chunk(j)], lambda j: kq_fr.at[1 + j, pl.ds(8, 32)])
-    load(2, lambda j: f_coeff.at[0, :, chunk(j)], lambda j: f_k.at[1 + j, pl.ds(8, 32)])
-    load(3, lambda j: f_start.at[0, :, chunk(j)], lambda j: f_v.at[1 + j, pl.ds(8, 32)])
-    load(4, lambda j: f_source.at[0, :, chunk(j)], lambda j: f_src.at[j])
-    load(5, lambda j: c_source.at[:, chunk(j)], lambda j: src_c.at[j])
-    load(6, lambda j: c_coeff.at[:, chunk(j)], lambda j: k_fr.at[5 + j, pl.ds(24, 32)])
+    load(0, lambda j: c_start.at[:, chunk(j)], lambda j: s_fr.at[1 + j, pl.ds(8, 32)], s_fr.at[pl.ds(1, 8), pl.ds(8, 32)])
+    load(1, lambda j: c_coeff.at[:, chunk(j)], lambda j: kq_fr.at[1 + j, pl.ds(8, 32)], kq_fr.at[pl.ds(1, 8), pl.ds(8, 32)])
+    load(2, lambda j: f_coeff.at[0, :, chunk(j)], lambda j: f_k.at[1 + j, pl.ds(8, 32)], f_k.at[pl.ds(1, 8), pl.ds(8, 32)])
+    load(3, lambda j: f_start.at[0, :, chunk(j)], lambda j: f_v.at[1 + j, pl.ds(8, 32)], f_v.at[pl.ds(1, 8), pl.ds(8, 32)])
+    load(4, lambda j: f_source.at[0, :, chunk(j)], lambda j: f_src.at[j], f_src)
+    load(5, lambda j: c_source.at[:, chunk(j)], lambda j: src_c.at[j], src_c)
+    load(6, lambda j: c_coeff.at[:, chunk(j)], lambda j: k_fr.at[5 + j, pl.ds(24, 32)], k_fr.at[pl.ds(5, 8), pl.ds(24, 32)])
 
     for q in range(5):
         for j in (4 - q, 13 + q):
@@ -454,13 +463,19 @@
             faces[2 * ox + oy] = faces[2 * ox + oy] + jnp.where(wanted, beside, 0.0)
 
     def to_mates(source, target, send_sem, recv_sem):
-        started = []
         for d in FAR_FIRST:
             other = lax.rem(mx + d, N_X)
-            started.append(
-                remote(source(other), target.at[mx], send_sem.at[d], recv_sem.at[d], (other, my))
-            )
-        return started
+            pltpu.make_async_remote_copy(
+                src_ref=source(other),
+                dst_ref=target.at[mx],
+                send_sem=send_sem.at[0],
+                recv_sem=recv_sem.at[0],
+                device_id=(other, my),
+                device_id_type=MESH,
+            ).start()
+        group = Group(target.at[pl.ds(0, N_X - 1)], send_sem.at[0], recv_sem.at[0])
+        sends.append(group)
+        return [group]
 
     for h in range(N_X):
         ghost_out[h] = faces[picks[h]]
@@ -784,6 +799,8 @@
     for j in range(8):
         b, q = j // 4, j % 4
         f_sm[j] = f_sm[j] + wide[32 * b : 32 * b + 32, 128 * q : 128 * q + 128]
+    for copy in sends:
+        copy.wait_send()
     for copy in settled:
         copy.wait_recv()
     tile = u_in[owner_x]
@@ -794,9 +811,6 @@
     wide = mapped(dup[0], m_four[...])
     for j in range(8):
         out[1, :, 128 * j : 128 * j + 128] = f_sm[j] + wide[:, 128 * j : 128 * j + 128]
-
-    for copy in sends:
-        copy.wait_send()
 
 
 def scratch():
@@ -816,8 +830,8 @@
     maps = [(2, 896, 128), (128, 1280), (512, 128), (128, 512), (2, 128, 256), (2, 256, 128)]
     result += [v(shape, BF16) for shape in maps + [(128, 1024)]]
     dma = pltpu.SemaphoreType.DMA
-    result += [dma((8, 8))] + [dma((8,))] * 2 + [dma((12,))] * 4 + [dma((N_X,))] * 4 + [dma((2,))] * 2
-    return result + [dma((N_X,))] * 4
+    result += [dma((9,))] + [dma((8,))] * 2 + [dma((12,))] * 4 + [dma((1,))] * 4 + [dma((2,))] * 2
+    return result + [dma((1,))] * 4
 
 
 def on_device(

time: 35.4 us -> 33.7 us (0.952)
  Pallas kernels: 33.9 us -> 32.2 us
    pallas_call x1, Pallas kernels: 33.9 us -> 32.2 us  [on_device(): pl.pallas_call(kernel, out_shape=jax.ShapeDtypeStruct((2, 32, 1024), F32)...]
where the time goes in v4:
time: 33.7 us; the launch traced here: 33.5 us
  Pallas kernels  32.2 us (96%)
  local copies, waits for them, and re-layouts  0.72 us (2%)
  between operations  0.64 us (2%)
    pallas_call x1, Pallas kernels, on_device(): pl.pallas_call(kernel, out_shape=jax.ShapeDtypeStruct((2, 32, 1024), F32)...  32.2 us
    slice x1, local copies, waits for them, and re-layouts, on_device(): return (both[0], both[1:])  0.72 us

profile of v4, /device:TPU:0, one launch (start us, length us, event | category | flops | bytes accessed | tf_op | source)
XLA Modules:
  0.0 33.5 jit_solution(3121385864386989298)
XLA Ops:
  0.6 32.2 %shard_map.95 = f32[2,32,1024]{2,1,0:T(8,128)S(1)} custom-call(s32[128]{0:T(128)} %pos_hbm.1, s32[3]{0:T(128)} %colours_hbm.1, f32[32,1024]{1,0:T(8,128)} %c_source.1, f32[32,1024]{1,0:T(8,128)} %c_coeff.1, f32[32,1024]{1,0:T(8,128)} %c_start.1, f32[1,32,1024]{2,1,0:T(8,128)} %f_source.1, f32[1,32,1024]{2,1,0:T(8,128)} %f_coeff.1, f32[1,32,1024]{2,1,0:T(8,128)} %f_start.1), custom_call_target="tpu_custom_call" | custom-call | tf_op jit(solution)/shard_map/pallas_call | solution.py:849
  32.8 0.7 %fusion = (f32[1,32,1024]{2,1,0:T(8,128)}, f32[32,1024]{1,0:T(8,128)}) fusion(f32[2,32,1024]{2,1,0:T(8,128)S(1)} %shard_map.95), kind=kLoop, calls=%fused_computation.1 | loop fusion | bytes 524288 | tf_op jit(solution)/shard_map/slice | solution.py:873

commit v5 on v4

--- a/solution.py
+++ b/solution.py
@@ -91,12 +91,15 @@
     def __init__(self, span, send_sem, recv_sem):
         self.sent = pltpu.make_async_copy(span, span, send_sem)
         self.landed = pltpu.make_async_copy(span, span, recv_sem)
+        self.left = False
 
     def wait_recv(self):
         self.landed.wait()
 
     def wait_send(self):
-        self.sent.wait()
+        if not self.left:
+            self.sent.wait()
+        self.left = True
 
 
 def put(ref, mask):
@@ -387,21 +390,22 @@
         return started
 
     def deep_y(ref, depth, send_sem, recv_sem):
-        started = []
         for q in range(depth):
             rows = pl.ds(8 + 4 * q, 64 - 8 * q)
             for side, (source, target) in enumerate(((5 + q, 13 + q), (12 - q, 4 - q))):
-                at = 2 + 2 * q + side
-                started.append(
-                    remote(
-                        ref.at[source, rows],
-                        ref.at[target, rows],
-                        send_sem.at[at],
-                        recv_sem.at[at],
-                        around[2 + side],
-                    )
-                )
-        return started
+                pltpu.make_async_remote_copy(
+                    src_ref=ref.at[source, rows],
+                    dst_ref=ref.at[target, rows],
+                    send_sem=send_sem.at[2],
+                    recv_sem=recv_sem.at[2],
+                    device_id=around[2 + side],
+                    device_id_type=MESH,
+                ).start()
+        total = 2 * sum(64 - 8 * q for q in range(depth))
+        span = ref.at[pl.ds(1, 8), pl.ds(8, total // 8)]
+        group = Group(span, send_sem.at[2], recv_sem.at[2])
+        sends.append(group)
+        return [group]
 
     deep_k = deep_x(k_fr, 17, sem_sk, sem_rk)
 
@@ -537,7 +541,7 @@
     def _():
         k_fr[5:13, 56:73] = jnp.zeros((8, 17, 128), F32)
 
-    deep_k += deep_y(k_fr, 5, sem_sk, sem_rk)
+    deep_k = deep_y(k_fr, 5, sem_sk, sem_rk)
 
     k = iota((128, 1280), 0)
     c = iota((128, 1280), 1)
@@ -594,7 +598,9 @@
     box_in[mx] = box_out[...]
     for copy in deep_r:
         copy.wait_recv()
-    deep_r += deep_y(r_fr, 4, sem_sr, sem_rr)
+    for copy in deep_r:
+        copy.wait_send()
+    deep_r = deep_y(r_fr, 4, sem_sr, sem_rr)
 
     zero_pads(wx, 8, 72)
     zero_pads(wy, 8, 72)
@@ -830,7 +836,7 @@
     maps = [(2, 896, 128), (128, 1280), (512, 128), (128, 512), (2, 128, 256), (2, 256, 128)]
     result += [v(shape, BF16) for shape in maps + [(128, 1024)]]
     dma = pltpu.SemaphoreType.DMA
-    result += [dma((9,))] + [dma((8,))] * 2 + [dma((12,))] * 4 + [dma((1,))] * 4 + [dma((2,))] * 2
+    result += [dma((9,))] + [dma((8,))] * 2 + [dma((3,))] * 4 + [dma((1,))] * 4 + [dma((2,))] * 2
     return result + [dma((1,))] * 4
 
 

time: 33.7 us -> 33.4 us (level)
  Pallas kernels: 32.2 us -> 31.8 us
where the time goes in v5:
time: 33.4 us; the launch traced here: 33.2 us
  Pallas kernels  31.8 us (95%)
  local copies, waits for them, and re-layouts  0.72 us (2%)
  between operations  0.64 us (2%)
    pallas_call x1, Pallas kernels, on_device(): pl.pallas_call(kernel, out_shape=jax.ShapeDtypeStruct((2, 32, 1024), F32)...  31.8 us
    slice x1, local copies, waits for them, and re-layouts, on_device(): return (both[0], both[1:])  0.72 us

profile of v5, /device:TPU:0, one launch (start us, length us, event | category | flops | bytes accessed | tf_op | source)
XLA Modules:
  0.0 33.2 jit_solution(14270973134700942591)
XLA Ops:
  0.6 31.8 %shard_map.95 = f32[2,32,1024]{2,1,0:T(8,128)S(1)} custom-call(s32[128]{0:T(128)} %pos_hbm.1, s32[3]{0:T(128)} %colours_hbm.1, f32[32,1024]{1,0:T(8,128)} %c_source.1, f32[32,1024]{1,0:T(8,128)} %c_coeff.1, f32[32,1024]{1,0:T(8,128)} %c_start.1, f32[1,32,1024]{2,1,0:T(8,128)} %f_source.1, f32[1,32,1024]{2,1,0:T(8,128)} %f_coeff.1, f32[1,32,1024]{2,1,0:T(8,128)} %f_start.1), custom_call_target="tpu_custom_call" | custom-call | tf_op jit(solution)/shard_map/pallas_call | solution.py:855
  32.5 0.7 %fusion = (f32[1,32,1024]{2,1,0:T(8,128)}, f32[32,1024]{1,0:T(8,128)}) fusion(f32[2,32,1024]{2,1,0:T(8,128)S(1)} %shard_map.95), kind=kLoop, calls=%fused_computation.1 | loop fusion | bytes 524288 | tf_op jit(solution)/shard_map/slice | solution.py:879

commit v6 on v5

--- a/solution.py
+++ b/solution.py
@@ -376,18 +376,19 @@
 
     def deep_x(ref, width, send_sem, recv_sem):
         blocks = pl.ds(5, 8)
-        started = []
         for side, (source, target) in enumerate(((24, 56), (56 - width, 24 - width))):
-            started.append(
-                remote(
-                    ref.at[blocks, pl.ds(source, width)],
-                    ref.at[blocks, pl.ds(target, width)],
-                    send_sem.at[side],
-                    recv_sem.at[side],
-                    around[side],
-                )
-            )
-        return started
+            pltpu.make_async_remote_copy(
+                src_ref=ref.at[blocks, pl.ds(source, width)],
+                dst_ref=ref.at[blocks, pl.ds(target, width)],
+                send_sem=send_sem.at[0],
+                recv_sem=recv_sem.at[0],
+                device_id=around[side],
+                device_id_type=MESH,
+            ).start()
+        span = ref.at[blocks, pl.ds(8, 2 * width)]
+        group = Group(span, send_sem.at[0], recv_sem.at[0])
+        sends.append(group)
+        return [group]
 
     def deep_y(ref, depth, send_sem, recv_sem):
         for q in range(depth):
@@ -695,10 +696,17 @@
     for ye in (1, 2):
         for sx in range(4):
             boxes[ye, sx] = box_in[jnp.maximum(found[4 * ye + sx], 0)]
-    beside = [
-        remote(boxes.at[1], boxes.at[3], sem_s3.at[0], sem_r3.at[0], around[2]),
-        remote(boxes.at[2], boxes.at[0], sem_s3.at[1], sem_r3.at[1], around[3]),
-    ]
+    for source, target, device in ((1, 3, around[2]), (2, 0, around[3])):
+        pltpu.make_async_remote_copy(
+            src_ref=boxes.at[source],
+            dst_ref=boxes.at[target],
+            send_sem=sem_s3.at[0],
+            recv_sem=sem_r3.at[0],
+            device_id=device,
+            device_id_type=MESH,
+        ).start()
+    beside = [Group(boxes.at[pl.ds(0, 2)], sem_s3.at[0], sem_r3.at[0])]
+    sends += beside
 
     def compose(ye):
         for oz in range(2):

time: 33.4 us -> 33.4 us (level)
  no operation moved by 1% of the time
where the time goes in v6:
time: 33.4 us; the launch traced here: 33.2 us
  Pallas kernels  31.8 us (95%)
  local copies, waits for them, and re-layouts  0.72 us (2%)
  between operations  0.64 us (2%)
    pallas_call x1, Pallas kernels, on_device(): pl.pallas_call(kernel, out_shape=jax.ShapeDtypeStruct((2, 32, 1024), F32)...  31.8 us
    slice x1, local copies, waits for them, and re-layouts, on_device(): return (both[0], both[1:])  0.72 us

profile of v6, /device:TPU:0, one launch (start us, length us, event | category | flops | bytes accessed | tf_op | source)
XLA Modules:
  0.0 33.2 jit_solution(12907991026488481420)
XLA Ops:
  0.6 31.8 %shard_map.95 = f32[2,32,1024]{2,1,0:T(8,128)S(1)} custom-call(s32[128]{0:T(128)} %pos_hbm.1, s32[3]{0:T(128)} %colours_hbm.1, f32[32,1024]{1,0:T(8,128)} %c_source.1, f32[32,1024]{1,0:T(8,128)} %c_coeff.1, f32[32,1024]{1,0:T(8,128)} %c_start.1, f32[1,32,1024]{2,1,0:T(8,128)} %f_source.1, f32[1,32,1024]{2,1,0:T(8,128)} %f_coeff.1, f32[1,32,1024]{2,1,0:T(8,128)} %f_start.1), custom_call_target="tpu_custom_call" | custom-call | tf_op jit(solution)/shard_map/pallas_call | solution.py:863
  32.5 0.7 %fusion = (f32[1,32,1024]{2,1,0:T(8,128)}, f32[32,1024]{1,0:T(8,128)}) fusion(f32[2,32,1024]{2,1,0:T(8,128)S(1)} %shard_map.95), kind=kLoop, calls=%fused_computation.1 | loop fusion | bytes 524288 | tf_op jit(solution)/shard_map/slice | solution.py:887
